TPU v7x, 32 devices: a whole 2x2x4 slice. The times are simulated.
32 devices in a mesh: grp: 16 (over z, x, core), tp: 2 (over y).
Axes of the slice: x: 2, y: 2, z: 4, core: 2. Of those that a mesh axis runs over, the one named last changes fastest.
Arguments:
- activations: bfloat16 [4096, 5120], P('grp', 'tp'), may hold values from -6 to 6
- cotangent: bfloat16 [4096, 512], P('grp'), may hold values from -1.5 to 1.5
- advantage: int32 [16], replicated, may hold values from -512 to 512
- seq_len: int32 [16], replicated, may hold values from 64 to 256, as said below
- key_master: float32 [2, 2560, 512], P('tp', 'grp'), may hold values from -0.078125 to 0.078125
- moment_one: float32 [2, 2560, 512], P('tp', 'grp'), may hold values from -3 to 3
- moment_two: float32 [2, 2560, 512], P('tp', 'grp'), may hold values from 0.1 to 2
- decode_hidden: bfloat16 [16, 4, 5120], P('grp'), may hold values from -6 to 6
- queries: bfloat16 [16, 4, 2560], P('grp', None, 'tp'), may hold values from -34 to 34
- cache_keys: bfloat16 [16, 2048, 512], P('grp', None, 'tp'), may hold values from -6 to 6
- cache_values: bfloat16 [16, 2048, 512], P('grp', None, 'tp'), may hold values from -6 to 6
- cache_len: int32 [16], P('grp'), may hold values from 2 to 2048, as said below
- value_weight: bfloat16 [5120, 512], P(None, 'tp'), may hold values from -0.078125 to 0.078125
Outputs:
- master_new: float32 [2, 2560, 512], P('tp', 'grp')
- moment_one_new: float32 [2, 2560, 512], P('tp', 'grp')
- moment_two_new: float32 [2, 2560, 512], P('tp', 'grp')
- new_keys: bfloat16 [16, 4, 512], P('grp', None, 'tp')
- new_values: bfloat16 [16, 4, 512], P('grp', None, 'tp')
- attention: bfloat16 [16, 4, 2560], P('grp', None, 'tp')
Inputs may be any that keep to these rules, and one draw needn't show every extreme that they name: `seq_len`: the first sequence is full. `cache_len`: row 0 has a full cache.
All inputs are finite; a program needn't handle non-finite values.
Results may differ from a plain program's by a relative error of at most 0.0044.
The roundings to bfloat16 on the way count: a program that leaves them out, or rounds other values in their place, can miss the bound.
Values may be sent and summed in bfloat16 or wider, within the bound.
A program may use at most 64 MiB of HBM per device.

v0:
```python
import math

import jax
import jax.numpy as jnp
from jax import lax
from jax.sharding import PartitionSpec as P

HD = 128
GQA = 5
SEQ = 256


def attend(queries, cache_keys, cache_values, cache_len, new_keys, new_values):
    rows, steps, width = queries.shape
    length = cache_keys.shape[1]
    heads_kv = cache_keys.shape[2] // HD
    inverse = 1.0 / math.sqrt(HD)
    shaped_q = queries.reshape(rows, steps, heads_kv, GQA, HD)
    keys_c = cache_keys.reshape(rows, length, heads_kv, HD)
    vals_c = cache_values.reshape(rows, length, heads_kv, HD)
    keys_n = new_keys.reshape(rows, steps, heads_kv, HD)
    vals_n = new_values.reshape(rows, steps, heads_kv, HD)
    score_c = (
        jnp.einsum("rsgqd,rcgd->rgsqc", shaped_q, keys_c, preferred_element_type=jnp.float32)
        * inverse
    )
    score_n = (
        jnp.einsum("rsgqd,rtgd->rgsqt", shaped_q, keys_n, preferred_element_type=jnp.float32)
        * inverse
    )
    valid = jnp.arange(length, dtype=jnp.int32)[None, :] < cache_len[:, None]
    score_c = jnp.where(valid[:, None, None, None, :], score_c, -jnp.inf)
    causal = (
        jnp.arange(steps, dtype=jnp.int32)[None, :] <= jnp.arange(steps, dtype=jnp.int32)[:, None]
    )
    score_n = jnp.where(causal[None, None, :, None, :], score_n, -jnp.inf)
    top = jnp.maximum(jnp.max(score_c, axis=-1), jnp.max(score_n, axis=-1))
    exp_c = jnp.exp(score_c - top[..., None])
    exp_n = jnp.exp(score_n - top[..., None])
    total = jnp.sum(exp_c, axis=-1) + jnp.sum(exp_n, axis=-1)
    probs_c = (exp_c / total[..., None]).astype(jnp.bfloat16)
    probs_n = (exp_n / total[..., None]).astype(jnp.bfloat16)
    mixed = jnp.einsum("rgsqc,rcgd->rsgqd", probs_c, vals_c, preferred_element_type=jnp.float32)
    mixed = mixed + jnp.einsum(
        "rgsqt,rtgd->rsgqd", probs_n, vals_n, preferred_element_type=jnp.float32
    )
    return mixed.astype(jnp.bfloat16).reshape(rows, steps, width)


def shards(
    activations,
    cotangent,
    advantage,
    seq_len,
    key_master,
    moment_one,
    moment_two,
    decode_hidden,
    queries,
    cache_keys,
    cache_values,
    cache_len,
    value_weight,
):
    tok_rows = activations.shape[0]
    quarter_rows = activations.shape[1]
    groups = lax.axis_size("grp")
    sequences = seq_len.shape[0]
    position = lax.axis_index("grp") * tok_rows + jnp.arange(tok_rows, dtype=jnp.int32)
    seq_index = position // SEQ
    within = position % SEQ
    onehot = seq_index[:, None] == jnp.arange(sequences, dtype=jnp.int32)[None, :]
    length_tok = jnp.sum(jnp.where(onehot, seq_len[None, :], 0), axis=1)
    adv_tok = jnp.sum(jnp.where(onehot, advantage[None, :], 0), axis=1).astype(jnp.float32) / 256.0
    scale = jnp.where(within < length_tok, adv_tok, jnp.float32(0.0)) / sequences
    weighted = (cotangent.astype(jnp.float32) * scale[:, None]).astype(jnp.bfloat16)
    own_rows = key_master.shape[1]
    padded = jnp.pad(activations, ((0, 0), (0, own_rows * groups - quarter_rows)))
    gradient = lax.psum_scatter(
        lax.dot_general(
            padded, weighted, (((0,), (0,)), ((), ())), preferred_element_type=jnp.float32
        ),
        "grp",
        scatter_dimension=0,
        tiled=True,
    )
    gradient = gradient.reshape(key_master.shape)
    corr_one = 1.0 - 0.9**10
    corr_two = 1.0 - 0.95**10
    moment_one_new = 0.9 * moment_one + 0.1 * gradient
    moment_two_new = 0.95 * moment_two + 0.05 * gradient * gradient
    master_new = key_master - 0.005 * (moment_one_new / corr_one) / (
        jnp.sqrt(moment_two_new / corr_two) + 1e-08
    )
    relay = master_new.astype(jnp.bfloat16)
    pieces = lax.all_to_all(relay, "tp", split_axis=2, concat_axis=0, tiled=True)
    columns = lax.all_gather(pieces, "grp", axis=1, tiled=True)
    weight_cols = columns[:, :quarter_rows].reshape(-1, columns.shape[2])
    rows, steps, width = decode_hidden.shape
    flat_hidden = decode_hidden.reshape(rows * steps, width)
    new_keys = (
        jnp.dot(flat_hidden, weight_cols, preferred_element_type=jnp.float32)
        .astype(jnp.bfloat16)
        .reshape(rows, steps, -1)
    )
    new_values = (
        jnp.dot(flat_hidden, value_weight, preferred_element_type=jnp.float32)
        .astype(jnp.bfloat16)
        .reshape(rows, steps, -1)
    )
    attention = attend(queries, cache_keys, cache_values, cache_len, new_keys, new_values)
    return (master_new, moment_one_new, moment_two_new, new_keys, new_values, attention)


def solution(mesh):
    placed = (
        P("grp", "tp"),
        P("grp", None),
        P(),
        P(),
        P("tp", "grp", None),
        P("tp", "grp", None),
        P("tp", "grp", None),
        P("grp", None, None),
        P("grp", None, "tp"),
        P("grp", None, "tp"),
        P("grp", None, "tp"),
        P("grp"),
        P(None, "tp"),
    )
    return jax.shard_map(
        shards,
        mesh=mesh,
        in_specs=placed,
        out_specs=(
            P("tp", "grp", None),
            P("tp", "grp", None),
            P("tp", "grp", None),
            P("grp", None, "tp"),
            P("grp", None, "tp"),
            P("grp", None, "tp"),
        ),
        check_vma=False,
    )
```

profile of v0, /device:TPU:0, one launch (start us, length us, event | category | flops | bytes accessed | tf_op | source)
XLA Modules:
  0.0 175.0 jit_solution(2456516851904867292)
XLA Ops:
  7.2 0.9 select_reduce_fusion.1
  8.2 4.7 %convolution_bitcast_fusion = f32[2560,512]{0,1:T(8,128)} fusion(bf16[256,2560]{1,0:T(8,128)(2,1)} %param.13, bf16[256,512]{1,0:T(8,128)(2,1)} %param.14, f32[256]{0:T(256)S(1)} %fusion.23), kind=kOutput, calls=%fused_computation | convolution fusion | flops 671481856 | bytes 6816768 | tf_op jit(solution)/shard_map/dot_general | solution.py:80
  12.9 5.9 %copy.117 = f32[2560,512]{1,0:T(8,128)} copy(f32[2560,512]{0,1:T(8,128)} %convolution_bitcast_fusion) | data formatting | bytes 10485760
  18.9 0.9 copy-done.3
  19.8 1.0 copy.92
  20.8 1.0 copy.93
  21.8 2.0 %copy.94 = f32[1,160,512]{1,2,0:T(8,128)} copy(f32[1,160,512]{2,1,0:T(8,128)} %param.17) | data formatting | bytes 655360 | tf_op args[4]
  23.8 76.3 %reduce-scatter.4.cloned.1.call-done = f32[160,512]{1,0:T(8,128)} async-done(((f32[2560,512]{1,0:T(8,128)}), f32[160,512]{1,0:T(8,128)}) %reduce-scatter.4.cloned.1.call-update) | async-done | bytes 327696
  100.1 2.0 %copy.118 = f32[160,512]{0,1:T(8,128)} copy(f32[160,512]{1,0:T(8,128)} %reduce-scatter.4.cloned.1.call-done) | data formatting | bytes 655360
  102.1 2.9 %fusion.24 = (bf16[1,160,512]{1,2,0:T(8,128)(2,1)S(1)}, f32[1,160,512]{1,2,0:T(8,128)}, f32[1,160,512]{1,2,0:T(8,128)}, f32[1,160,512]{1,2,0:T(8,128)S(1)}) fusion(f32[1,160,512]{1,2,0:T(8,128)} %copy.94, f32[160,512]{0,1:T(8,128)} %copy.118, f32[1,160,512]{1,2,0:T(8,128)} %copy.92, f32[1,160,512]{1,2,0:T(8,128)} %copy.93), kind=kLoop, calls=%fused_computation.52 | loop fusion | flops 1064960 | bytes 2457600 | tf_op jit(solution)/shard_map/convert_element_type | solution.py:95
  104.9 1.2 copy.134
  106.1 0.5 broadcast.126
  106.6 3.2 %reduce.8 = bf16[512,160]{1,0:T(8,128)(2,1)S(1)} reduce(bf16[512,1,160]{2,1,0:T(2,128)(2,1)} %bitcast.64, bf16[]{:T(256)} %broadcast.126), dimensions={1}, to_apply=%bitcast.60.reduce_sub_computation | reduce | bytes 327682
  109.8 1.1 reshape.198
  110.9 8.1 %all_to_all.18 = bf16[2,2,20480]{2,1,0:T(2,128)(2,1)S(1)} all-to-all(bf16[2,2,20480]{2,1,0:T(2,128)(2,1)} %reshape.198), channel_id=1, replica_groups=mesh['grp'=16,'tp'=2] {'tp'}, dimensions={0} | all-to-all | bytes 327680 | tf_op jit(solution)/shard_map/all_to_all | solution.py:96
  119.0 1.1 reshape.199
  120.1 1.2 copy.96
  121.3 0.7 all_to_all.14
  122.1 2.1 %reshape.185 = bf16[2048,2,128]{2,1,0:T(2,128)(2,1)} reshape(bf16[1,2048,256]{2,1,0:T(8,128)(2,1)} %param.22) | data formatting | bytes 2097152 | tf_op jit(solution)/shard_map/reshape.3
  124.9 2.2 %reshape.187 = bf16[2048,2,128]{2,1,0:T(2,128)(2,1)} reshape(bf16[1,2048,256]{2,1,0:T(8,128)(2,1)} %param.23) | data formatting | bytes 2097152 | tf_op jit(solution)/shard_map/reshape.21
  127.1 2.5 %fusion.26 = (f32[2,4,5]{2,1,0:T(4,128)S(1)}, f32[2,4,5,2048]{3,2,1,0:T(8,128)}) fusion(bf16[2048,2,128,1]{2,1,0,3:T(2,128)(2,1)} %bitcast.63, bf16[4,2,5,128]{3,2,1,0:T(8,128)(2,1)S(1)} %reshape.184, pred[2048]{0:T(1024)(128)(4,1)S(1)} %iota_compare_fusion.1), kind=kOutput, calls=%fused_computation.53 | convolution fusion | flops 21217240 | bytes 1388704 | tf_op jit(solution)/shard_map/rsgqd,rcgd->rgsqc/dot_general | solution.py:24
  129.6 0.4 convolution_convert_fusion
  130.0 2.0 %copy.106 = f32[1,160,512]{2,1,0:T(8,128)} copy(f32[1,160,512]{1,2,0:T(8,128)} %get-tuple-element.45) | data formatting | bytes 655360
  132.0 1.9 %copy.107 = f32[1,160,512]{2,1,0:T(8,128)} copy(f32[1,160,512]{1,2,0:T(8,128)} %get-tuple-element.46) | data formatting | bytes 655360
  133.9 0.9 copy.108
  134.8 28.6 %all-gather.3.cloned.1.call-done = bf16[2,1,2560,256]{3,0,1,2:T(2,128)(2,1)} async-done(((bf16[2,1,160,256]{3,0,1,2:T(2,128)(2,1)}), bf16[2,1,2560,256]{3,0,1,2:T(2,128)(2,1)}) %all-gather.3.cloned.1.call-update) | async-done | bytes 2621456 | tf_op jit(solution)/shard_map/all_gather | solution.py:97
  163.4 2.1 %copy.98 = bf16[2,1,2560,256]{3,2,0,1:T(8,128)(2,1)S(1)} copy(bf16[2,1,2560,256]{3,0,1,2:T(2,128)(2,1)} %all-gather.3.cloned.1.call-done) | data formatting | bytes 5242880 | tf_op jit(solution)/shard_map/all_gather | solution.py:97
  165.5 0.4 convolution_convert_fusion.1
  166.3 0.3 copy-done.1
  166.6 0.2 fusion.9
  166.9 0.4 convolution_bitcast_fusion.1
  167.5 0.6 reshape.189
  (31 shorter events, 0.8 us)
Async XLA Ops:
  7.2 122.4 %copy-start = (bf16[5120,256]{1,0:T(8,128)(2,1)S(1)}, bf16[5120,256]{1,0:T(8,128)(2,1)}, u32[]{:S(2)}) copy-start(bf16[5120,256]{1,0:T(8,128)(2,1)} %param.25) | copy-start | bytes 7864324
  7.2 92.9 %reduce-scatter.4.cloned.1.call-start = ((), (), s32[]{:S(2)}) async-start(), calls=%async_computation.3 | async-start | bytes 5570560
  18.8 1.0 copy-start.3
  18.8 2.0 %copy-start.4 = (f32[1,160,512]{2,1,0:T(8,128)S(1)}, f32[1,160,512]{2,1,0:T(8,128)}, u32[]{:S(2)}) copy-start(f32[1,160,512]{2,1,0:T(8,128)} %param.19) | copy-start | bytes 983044
  18.8 144.6 %all-gather.3.cloned.1.call-start = ((), (), s32[]{:S(2)}) async-start(), calls=%async_computation.2 | async-start | bytes 2785280 | tf_op jit(solution)/shard_map/all_gather | solution.py:97
  104.9 17.1 %copy-start.6 = (bf16[1,4,1280]{2,1,0:T(4,128)(2,1)S(1)}, bf16[1,4,1280]{2,1,0:T(4,128)(2,1)}, u32[]{:S(2)}) copy-start(bf16[1,4,1280]{2,1,0:T(4,128)(2,1)} %param.21) | copy-start | bytes 30724
  122.1 7.5 %copy-start.5 = (bf16[1,4,5120]{2,1,0:T(4,128)(2,1)S(1)}, bf16[1,4,5120]{2,1,0:T(4,128)(2,1)}, u32[]{:S(2)}) copy-start(bf16[1,4,5120]{2,1,0:T(4,128)(2,1)} %param.20) | copy-start | bytes 122884
  130.0 37.3 %copy-start.7 = (bf16[4,256]{1,0:T(4,128)(2,1)}, bf16[4,256]{1,0:T(4,128)(2,1)S(1)}, u32[]{:S(2)}) copy-start(bf16[4,256]{1,0:T(4,128)(2,1)S(1)} %convolution_convert_fusion) | copy-start | bytes 6148
  165.5 1.0 copy-start.1
  165.5 1.4 copy-start.2
  166.0 2.1 %copy-start.8 = (bf16[256,4]{0,1:T(4,128)(2,1)}, bf16[256,4]{0,1:T(4,128)(2,1)S(1)}, u32[]{:S(2)}) copy-start(bf16[256,4]{0,1:T(4,128)(2,1)S(1)} %convolution_convert_fusion.1) | copy-start | bytes 6148
Sparse Core Ops, SparseCore 0:
  19.0 81.0 reduce-scatter.3
  122.2 41.2 all-gather.2
where the time goes:
time: 176 us; the launch traced here: 175 us
  waiting for transfers between devices  105 us (60%)
  local copies, waits for them, and re-layouts  30.9 us (18%)
  between operations  14.8 us (8%)
  matrix products  8.86 us (5%)
  blocking collectives  8.06 us (5%)
  other arithmetic  7.28 us (4%)
    unnamed x3, waiting for transfers between devices  76.3 us
    all_gather x1, waiting for transfers between devices, shards(): columns = lax.all_gather(pieces, 'grp', axis=1, tiled=True)  28.6 us
    unnamed x29, local copies, waits for them, and re-layouts  20.8 us
    all_to_all x1, blocking collectives, shards(): lax.all_to_all(relay, 'tp', split_axis=2, concat_axis=0, tiled=True)  8.06 us
    dot_general x1, matrix products, shards(): lax.dot_general(padded, weighted, (((0,), (0,)), ((), ())), preferred_ele...  4.71 us
    another operation x3, local copies, waits for them, and re-layouts  4.32 us
  transfers between devices with their start and end apart: 2, of which 2 were waited for; matrix products, arithmetic and copies ran while one was open for 9% of the time, Pallas kernels for 0%

commit v1 on v0

--- a/solution.py
+++ b/solution.py
@@ -1,8 +1,11 @@
+import functools
 import math
 
 import jax
 import jax.numpy as jnp
 from jax import lax
+from jax.experimental import pallas as pl
+from jax.experimental.pallas import tpu as pltpu
 from jax.sharding import PartitionSpec as P
 
 HD = 128
@@ -47,7 +50,7 @@
     return mixed.astype(jnp.bfloat16).reshape(rows, steps, width)
 
 
-def shards(
+def plain_shards(
     activations,
     cotangent,
     advantage,
@@ -112,6 +115,388 @@
     return (master_new, moment_one_new, moment_two_new, new_keys, new_values, attention)
 
 
+MESH = pl.DeviceIdType.MESH
+F32 = jnp.float32
+BF16 = jnp.bfloat16
+
+
+def fused(
+    dims,
+    act_ref, cot_ref, adv_ref, len_ref, master_ref, one_ref, two_ref, hid_ref, hid_own_ref,
+    dec_ref, query_ref, ck_ref, cv_ref, clen_ref, vw_ref,
+    master_out, one_out, two_out, keys_out, values_out, att_out,
+    part, core_in, acc, x_out, x_in, z_out, z_in,
+    hid, hid_rows, spread, y_part, y_core, y_x, y_xin, y_z, y_zin, y_t, y_tin,
+    ck, cv, vw, q_rows, scores, new_k, new_v, rows16, att,
+    local_sem, core_sem, x_sem, z_sem, hz_sem, hx_sem, yc_sem, yz_sem, yt_sem,
+):
+    groups, tps, steps = dims
+    depth = groups // 4
+    me = lax.axis_index("grp")
+    t = lax.axis_index("tp")
+    core = lax.rem(me, 2)
+    x = lax.rem(lax.div(me, 2), 2)
+    z = lax.div(me, 4)
+    other_core, other_x = 1 - core, 1 - x
+    core_dev = (z * 4 + x * 2 + other_core, t)
+    x_dev = (z * 4 + other_x * 2 + core, t)
+
+    def z_dev(j):
+        return (lax.rem(z + j, depth) * 4 + x * 2 + core, t)
+
+    def t_dev(i):
+        return (me, lax.rem(t + i, tps))
+
+    partners = [core_dev, x_dev]
+    partners += [z_dev(j) for j in range(1, depth)] + [t_dev(i) for i in range(1, tps)]
+    sent = []
+
+    def remote(src, dst, sems, slot, device):
+        return pltpu.make_async_remote_copy(
+            src_ref=src, dst_ref=dst, send_sem=sems.at[0, slot], recv_sem=sems.at[1, slot],
+            device_id=device, device_id_type=MESH,
+        )
+
+    def send(copy):
+        copy.start()
+        sent.append(copy)
+        return copy
+
+    load_k = pltpu.make_async_copy(ck_ref, ck, local_sem.at[0])
+    load_v = pltpu.make_async_copy(cv_ref, cv, local_sem.at[1])
+    load_w = pltpu.make_async_copy(vw_ref, vw, local_sem.at[2])
+    load_k.start()
+    load_v.start()
+    load_w.start()
+
+    barrier = pltpu.get_barrier_semaphore()
+    for device in partners:
+        pl.semaphore_signal(barrier, inc=1, device_id=device, device_id_type=MESH)
+
+    tokens, width = act_ref.shape
+    sequences = len_ref.shape[1]
+    position = me * tokens + lax.broadcasted_iota(jnp.int32, (tokens, sequences), 0)
+    which = lax.broadcasted_iota(jnp.int32, (tokens, sequences), 1)
+    mine = lax.div(position, SEQ) == which
+    length = jnp.sum(jnp.where(mine, len_ref[...].astype(F32), 0.0), axis=1, keepdims=True)
+    advantage = jnp.sum(jnp.where(mine, adv_ref[...].astype(F32), 0.0), axis=1, keepdims=True)
+    within = lax.rem(
+        me * tokens + lax.broadcasted_iota(jnp.int32, (tokens, 1), 0), SEQ
+    ).astype(F32)
+    scale = jnp.where(within < length, advantage / 256.0, 0.0) / sequences
+    weighted = (cot_ref[...].astype(F32) * scale).astype(BF16)
+
+    chunk = width // depth
+    own = chunk // 4
+    kw = cot_ref.shape[1]
+    order = list(range(1, depth)) + [0]
+
+    core_copies = {}
+    waited = False
+    for j in order:
+        at = pl.multiple_of(lax.rem(z + j, depth) * chunk, 128)
+        product = lax.dot_general(
+            act_ref[:, pl.ds(at, chunk)], weighted, (((0,), (0,)), ((), ())),
+            preferred_element_type=F32,
+        )
+        part[j] = product.reshape(2, 2, own, kw)
+        if not waited:
+            pl.semaphore_wait(barrier, len(partners))
+            waited = True
+        core_copies[j] = send(
+            remote(part.at[j, :, other_core], core_in.at[j], core_sem, j, core_dev)
+        )
+
+    hid[0, 0, 0] = hid_own_ref[...]
+    hid_z = [
+        send(remote(hid_ref.at[lax.rem(z + j, depth)], hid.at[0, 0, j], hz_sem, j, z_dev(j)))
+        for j in range(1, depth)
+    ]
+
+    x_copies = {}
+    for j in order:
+        core_copies[j].wait_recv()
+        x_out[j] = (part[j, other_x, core] + core_in[j, other_x]).astype(BF16)
+        x_copies[j] = send(remote(x_out.at[j], x_in.at[j], x_sem, j, x_dev))
+        acc[j] = part[j, x, core] + core_in[j, x]
+
+    heads = ck.shape[1] // HD
+    gqa = GQA
+    for copy in hid_z:
+        copy.wait_recv()
+    hid_x = send(remote(hid.at[0, 0], hid.at[0, 1], hx_sem, 0, x_dev))
+
+    inverse = 1.0 / math.sqrt(HD)
+    cached = ck.shape[0]
+    q_rows[...] = jnp.zeros_like(q_rows)
+    query = query_ref[...].astype(F32)
+    for h in range(heads * gqa):
+        q_rows[h // gqa, pl.ds((h % gqa) * steps, steps)] = query[:, h * HD : (h + 1) * HD]
+
+    def cache_scores(g):
+        scores[g, :, pl.ds(0, cached)] = lax.dot_general(
+            q_rows[g].astype(BF16), ck[:, g * HD : (g + 1) * HD], (((1,), (1,)), ((), ())),
+            preferred_element_type=F32,
+        )
+
+
+    def project_values():
+        load_w.wait()
+        rows16[...] = jnp.zeros_like(rows16)
+        rows16[pl.ds(0, steps)] = jnp.dot(dec_ref[...], vw[...], preferred_element_type=F32)
+        new_v[...] = jnp.zeros_like(new_v)
+        new_v[pl.ds(0, 16)] = rows16[...].astype(BF16)
+        values_out[...] = rows16[pl.ds(0, steps)].astype(BF16)
+
+    load_k.wait()
+    z_copies = []
+    for turn, j in enumerate(order):
+        if turn < heads:
+            cache_scores(turn)
+        if turn == len(order) - 1:
+            for g in range(len(order), heads):
+                cache_scores(g)
+            project_values()
+        x_copies[j].wait_recv()
+        total = acc[j] + x_in[j].astype(F32)
+        if j == 0:
+            acc[0] = total
+        else:
+            z_out[j - 1] = total.astype(BF16)
+            z_copies.append(
+                send(remote(z_out.at[j - 1], z_in.at[j - 1], z_sem, j - 1, z_dev(j)))
+            )
+    hid_x.wait_recv()
+    hid_core = send(remote(hid.at[0], hid.at[1], hx_sem, 1, core_dev))
+    hid_core.wait_recv()
+    for c in range(2):
+        for b in range(2):
+            for j in range(depth):
+                at = ((c * 2 + b) * depth + j) * steps
+                hid_rows[pl.ds(at, steps)] = hid[c, b, j]
+    spread[...] = jnp.zeros_like(spread)
+    new_k[...] = jnp.zeros_like(new_k)
+
+    for copy in z_copies:
+        copy.wait_recv()
+    gradient = acc[0]
+    for j in range(1, depth):
+        gradient = gradient + z_in[j - 1].astype(F32)
+
+    corr_one = 1.0 - 0.9**10
+    corr_two = 1.0 - 0.95**10
+    one_new = 0.9 * one_ref[...] + 0.1 * gradient
+    two_new = 0.95 * two_ref[...] + 0.05 * gradient * gradient
+    master_new = master_ref[...] - 0.005 * (one_new / corr_one) / (
+        jnp.sqrt(two_new / corr_two) + 1e-08
+    )
+    one_out[...] = one_new
+    two_out[...] = two_new
+    master_out[...] = master_new
+
+    spread[pl.ds(pl.multiple_of((x * 2 + core) * own, 16), own)] = master_new.astype(BF16)
+    product = jnp.dot(hid_rows[...].astype(BF16), spread[...], preferred_element_type=F32)
+    half = product.shape[0] // 2
+    y_part[...] = product[half:]
+    copy = send(remote(y_part, y_core, yc_sem, 0, core_dev))
+    copy.wait_recv()
+    product = product[:half] + y_core[...]
+    half = half // 2
+    y_x[...] = product[half:]
+    copy = send(remote(y_x, y_xin, yc_sem, 1, x_dev))
+    copy.wait_recv()
+    product = product[:half] + y_xin[...]
+    copies = []
+    for j in range(1, depth):
+        y_z[j - 1] = product[j * steps : (j + 1) * steps]
+        copies.append(
+            send(remote(y_z.at[j - 1], y_zin.at[j - 1], yz_sem, j - 1, z_dev(depth - j)))
+        )
+    for copy in copies:
+        copy.wait_recv()
+    product = product[:steps]
+    for j in range(1, depth):
+        product = product + y_zin[j - 1]
+    columns = kw // tps
+    for i in range(tps):
+        y_t[i] = product[:, i * columns : (i + 1) * columns]
+    copies = [
+        send(remote(y_t.at[lax.rem(t + i, tps)], y_tin.at[i - 1], yt_sem, i - 1, t_dev(i)))
+        for i in range(1, tps)
+    ]
+    for copy in copies:
+        copy.wait_recv()
+    keys = y_t[t]
+    for i in range(1, tps):
+        keys = keys + y_tin[i - 1]
+    rows16[...] = jnp.zeros_like(rows16)
+    rows16[pl.ds(0, steps)] = keys
+    keys_out[...] = keys.astype(BF16)
+    new_k[pl.ds(0, 16)] = rows16[...].astype(BF16)
+
+    load_v.wait()
+    rows = q_rows.shape[1]
+    column = lax.broadcasted_iota(jnp.int32, (rows, cached), 1)
+    valid = column < clen_ref[0]
+    step = lax.rem(lax.broadcasted_iota(jnp.int32, (rows, HD), 0), steps)
+    causal = lax.broadcasted_iota(jnp.int32, (rows, HD), 1) <= step
+    for g in range(heads):
+        lanes = slice(g * HD, (g + 1) * HD)
+        score_n = lax.dot_general(
+            q_rows[g].astype(BF16), new_k[:, lanes], (((1,), (1,)), ((), ())),
+            preferred_element_type=F32,
+        )
+        score_c = jnp.where(valid, scores[g] * inverse, -jnp.inf)
+        score_n = jnp.where(causal, score_n * inverse, -jnp.inf)
+        top = jnp.maximum(
+            jnp.max(score_c, axis=1, keepdims=True), jnp.max(score_n, axis=1, keepdims=True)
+        )
+        exp_c = jnp.exp(score_c - top)
+        exp_n = jnp.exp(score_n - top)
+        total = jnp.sum(exp_c, axis=1, keepdims=True) + jnp.sum(exp_n, axis=1, keepdims=True)
+        mixed = jnp.dot(
+            (exp_c / total).astype(BF16), cv[:, lanes], preferred_element_type=F32
+        ) + jnp.dot((exp_n / total).astype(BF16), new_v[:, lanes], preferred_element_type=F32)
+        for i in range(gqa):
+            at = (g * gqa + i) * HD
+            att[:, at : at + HD] = mixed[i * steps : (i + 1) * steps]
+    att_out[...] = att[...].astype(BF16)
+
+    for copy in sent:
+        copy.wait_send()
+
+
+def fast_shards(
+    activations,
+    cotangent,
+    advantage,
+    seq_len,
+    key_master,
+    moment_one,
+    moment_two,
+    decode_hidden,
+    queries,
+    cache_keys,
+    cache_values,
+    cache_len,
+    value_weight,
+):
+    groups, tps = lax.axis_size("grp"), lax.axis_size("tp")
+    depth = groups // 4
+    tokens, width = activations.shape
+    own, kw = key_master.shape[1:]
+    chunk = width // depth
+    steps = decode_hidden.shape[1]
+    cached, kv_cols = cache_keys.shape[1:]
+    heads = kv_cols // HD
+    hidden = decode_hidden.reshape(steps, -1)
+    mine = lax.dynamic_slice_in_dim(hidden, lax.axis_index("tp") * width, width, 1)
+    mine = mine.reshape(steps, depth, chunk).transpose(1, 0, 2).astype(F32)
+    own_hidden = lax.dynamic_index_in_dim(mine, lax.axis_index("grp") // 4, 0, keepdims=False)
+    q_pad = -(-GQA * steps // 16) * 16
+    vmem = pl.BlockSpec(memory_space=pltpu.VMEM)
+    anywhere = pl.BlockSpec(memory_space=pl.ANY)
+    smem = pl.BlockSpec(memory_space=pltpu.SMEM)
+    dma = pltpu.SemaphoreType.DMA
+    rows = groups * steps
+    outs = pl.pallas_call(
+        functools.partial(fused, (groups, tps, steps)),
+        out_shape=(
+            jax.ShapeDtypeStruct((own, kw), F32),
+            jax.ShapeDtypeStruct((own, kw), F32),
+            jax.ShapeDtypeStruct((own, kw), F32),
+            jax.ShapeDtypeStruct((steps, kv_cols), BF16),
+            jax.ShapeDtypeStruct((steps, kv_cols), BF16),
+            jax.ShapeDtypeStruct((steps, queries.shape[2]), BF16),
+        ),
+        in_specs=[vmem] * 11 + [anywhere, anywhere, smem, anywhere],
+        out_specs=(vmem,) * 6,
+        scratch_shapes=[
+            pltpu.VMEM((depth, 2, 2, own, kw), F32),
+            pltpu.VMEM((depth, 2, own, kw), F32),
+            pltpu.VMEM((depth, own, kw), F32),
+            pltpu.VMEM((depth, own, kw), BF16),
+            pltpu.VMEM((depth, own, kw), BF16),
+            pltpu.VMEM((depth - 1, own, kw), BF16),
+            pltpu.VMEM((depth - 1, own, kw), BF16),
+            pltpu.VMEM((2, 2, depth, steps, chunk), F32),
+            pltpu.VMEM((rows, chunk), F32),
+            pltpu.VMEM((chunk, kw), BF16),
+            pltpu.VMEM((rows // 2, kw), F32),
+            pltpu.VMEM((rows // 2, kw), F32),
+            pltpu.VMEM((rows // 4, kw), F32),
+            pltpu.VMEM((rows // 4, kw), F32),
+            pltpu.VMEM((depth - 1, steps, kw), F32),
+            pltpu.VMEM((depth - 1, steps, kw), F32),
+            pltpu.VMEM((tps, steps, kw // tps), F32),
+            pltpu.VMEM((tps - 1, steps, kw // tps), F32),
+            pltpu.VMEM((cached, kv_cols), BF16),
+            pltpu.VMEM((cached, kv_cols), BF16),
+            pltpu.VMEM(value_weight.shape, BF16),
+            pltpu.VMEM((heads, q_pad, HD), F32),
+            pltpu.VMEM((heads, q_pad, cached), F32),
+            pltpu.VMEM((HD, kv_cols), BF16),
+            pltpu.VMEM((HD, kv_cols), BF16),
+            pltpu.VMEM((16, kv_cols), F32),
+            pltpu.VMEM((steps, queries.shape[2]), F32),
+            dma((3,)),
+            dma((2, depth)),
+            dma((2, depth)),
+            dma((2, depth)),
+            dma((2, depth)),
+            dma((2, 2)),
+            dma((2, 2)),
+            dma((2, depth)),
+            dma((2, tps)),
+        ],
+        compiler_params=pltpu.CompilerParams(
+            collective_id=0, has_side_effects=True, vmem_limit_bytes=56 * 1024 * 1024
+        ),
+        cost_estimate=pl.CostEstimate(
+            flops=2 * tokens * width * kw, bytes_accessed=8 * width * kw, transcendentals=0
+        ),
+    )(
+        activations,
+        cotangent,
+        advantage.reshape(1, -1),
+        seq_len.reshape(1, -1),
+        key_master[0],
+        moment_one[0],
+        moment_two[0],
+        mine,
+        own_hidden,
+        hidden,
+        queries[0],
+        cache_keys[0],
+        cache_values[0],
+        cache_len,
+        value_weight,
+    )
+    return tuple(out[None] for out in outs)
+
+
+def fits(activations, key_master, decode_hidden, cache_keys, value_weight):
+    groups, tps = lax.axis_size("grp"), lax.axis_size("tp")
+    own = key_master.shape[1]
+    return (
+        groups % 4 == 0
+        and groups >= 8
+        and tps >= 2
+        and own % 16 == 0
+        and own * groups == activations.shape[1]
+        and (4 * own) % 128 == 0
+        and decode_hidden.shape[0] == 1
+        and decode_hidden.shape[1] <= 16
+        and cache_keys.shape[1] % 128 == 0
+    )
+
+
+def shards(*args):
+    if fits(args[0], args[4], args[7], args[9], args[12]):
+        return fast_shards(*args)
+    return plain_shards(*args)
+
+
 def solution(mesh):
     placed = (
         P("grp", "tp"),

time: 176 us -> 56.8 us (0.32)
  waiting for transfers between devices: 105 us -> 0 us
  Pallas kernels: 0 us -> 44.2 us
  local copies, waits for them, and re-layouts: 30.9 us -> 10.3 us
  between operations: 14.8 us -> 1.31 us
  matrix products: 8.86 us -> 0 us
  blocking collectives: 8.06 us -> 0 us
  other arithmetic: 7.28 us -> 0.63 us
    unnamed x3 -> x0, waiting for transfers between devices: 76.3 us -> none
    pallas_call x0 -> x1, Pallas kernels: none -> 44.2 us  [fast_shards(): pl.pallas_call(functools.partial(fused, (groups, tps, steps)), out_shape=...]
    all_gather x1 -> x0, waiting for transfers between devices: 28.6 us -> none  [shards(): columns = lax.all_gather(pieces, 'grp', axis=1, tiled=True)]
    unnamed x29 -> x6, local copies, waits for them, and re-layouts: 20.8 us -> 8.95 us
    dot_general x7 -> x0, matrix products: 8.86 us -> none  [the longest x1 4.71 us: shards(): lax.dot_general(padded, weighted, (((0,), (0,)), ((), ())), preferred_ele...]
    all_to_all x1 -> x0, blocking collectives: 8.06 us -> none  [shards(): lax.all_to_all(relay, 'tp', split_axis=2, concat_axis=0, tiled=True)]
    another operation x3 -> x0, local copies, waits for them, and re-layouts: 4.32 us -> none
    unnamed x1 -> x0, other arithmetic: 3.18 us -> none
  transfers between devices with their start and end apart: 2 -> 0, of which waited for: 2 -> 0; matrix products, arithmetic and copies ran while one was open for 9% -> 0% of each run, Pallas kernels for 0% -> 0%
where the time goes in v1:
time: 56.8 us; the launch traced here: 56.4 us
  Pallas kernels  44.2 us (78%)
  local copies, waits for them, and re-layouts  10.3 us (18%)
  between operations  1.31 us (2%)
  other arithmetic  0.63 us (1%)
    pallas_call x1, Pallas kernels, fast_shards(): pl.pallas_call(functools.partial(fused, (groups, tps, steps)), out_shape=...  44.2 us
    unnamed x6, local copies, waits for them, and re-layouts  8.95 us

profile of v1, /device:TPU:0, one launch (start us, length us, event | category | flops | bytes accessed | tf_op | source)
XLA Modules:
  0.0 56.4 jit_solution(8888770406257763465)
XLA Ops:
  1.3 0.7 %constant_dynamic-slice_fusion = bf16[1,4,2560]{2,1,0:T(4,128)(2,1)S(1)} fusion(bf16[1,4,5120]{2,1,0:T(4,128)(2,1)} %param.20, s32[]{:T(128)S(6)} %select_n.12), kind=kLoop, calls=%fused_computation.2 | loop fusion | bytes 40964 | tf_op jit(solution)/shard_map/dynamic_slice | solution.py:393
  2.0 0.6 %convert_bitcast_fusion.hid_ref = f32[4,4,640]{2,1,0:T(4,128)} fusion(bf16[4,4,640]{2,0,1:T(4,128)(2,1)S(1)} %bitcast.29), kind=kLoop, calls=%fused_computation | loop fusion | flops 10240 | bytes 61440 | tf_op jit(solution)/shard_map/convert_element_type | solution.py:394
  2.7 0.6 %dynamic-slice_bitcast_fusion.hid_own_ref = f32[4,640]{1,0:T(4,128)} fusion(f32[4,4,640]{2,0,1:T(4,128)S(1)} %convert.1, s32[]{:T(128)S(6)} %select_n.14), kind=kLoop, calls=%fused_computation.1 | loop fusion | bytes 20484 | tf_op jit(solution)/shard_map/jit(dynamic_index_in_dim)/squeeze | solution.py:395
  3.3 44.2 %shard_map.172 = (f32[160,512]{1,0:T(8,128)}, f32[160,512]{1,0:T(8,128)}, f32[160,512]{1,0:T(8,128)}, bf16[4,256]{1,0:T(4,128)(2,1)}, bf16[4,256]{1,0:T(4,128)(2,1)}, /*index=5*/bf16[4,1280]{1,0:T(4,128)(2,1)}) custom-call(bf16[256,2560]{1,0:T(8,128)(2,1)} %act_ref.1, bf16[256,512]{1,0:T(8,128)(2,1)} %cot_ref.1, s32[1,16]{1,0:T(1,128)} %bitcast.36, ...), custom_call_target="tpu_custom_call" | custom-call | flops 671088640 | bytes 10485760 | tf_op jit(solution)/shard_map/pallas_call | solution.py:402
  47.4 1.7 %copy.26 = f32[1,160,512]{2,1,0:T(8,128)} copy(f32[1,160,512]{2,1,0:T(8,128)} %bitcast.28) | data formatting | bytes 655360
  49.2 1.7 %copy.27 = f32[1,160,512]{2,1,0:T(8,128)} copy(f32[1,160,512]{2,1,0:T(8,128)} %bitcast.27) | data formatting | bytes 655360
  50.9 1.7 %copy.28 = f32[1,160,512]{2,1,0:T(8,128)} copy(f32[1,160,512]{2,1,0:T(8,128)} %bitcast.26) | data formatting | bytes 655360
  52.6 1.2 %copy.29 = bf16[1,4,256]{2,1,0:T(4,128)(2,1)} copy(bf16[1,4,256]{2,1,0:T(4,128)(2,1)} %bitcast.35) | data formatting | bytes 4096
  53.8 1.3 %copy.30 = bf16[1,4,256]{2,1,0:T(4,128)(2,1)} copy(bf16[1,4,256]{2,1,0:T(4,128)(2,1)} %bitcast.34) | data formatting | bytes 4096
  55.1 1.3 %copy.31 = bf16[1,4,1280]{2,1,0:T(4,128)(2,1)} copy(bf16[1,4,1280]{2,1,0:T(4,128)(2,1)} %bitcast.33) | data formatting | bytes 20480
  (1 shorter events, 0.0 us)

commit v2 on v1

--- a/solution.py
+++ b/solution.py
@@ -122,7 +122,7 @@
 
 def fused(
     dims,
-    act_ref, cot_ref, adv_ref, len_ref, master_ref, one_ref, two_ref, hid_ref, hid_own_ref,
+    act_ref, cot_ref, adv_ref, len_ref, master_ref, one_ref, two_ref, hid_ref,
     dec_ref, query_ref, ck_ref, cv_ref, clen_ref, vw_ref,
     master_out, one_out, two_out, keys_out, values_out, att_out,
     part, core_in, acc, x_out, x_in, z_out, z_in,
@@ -207,7 +207,7 @@
             remote(part.at[j, :, other_core], core_in.at[j], core_sem, j, core_dev)
         )
 
-    hid[0, 0, 0] = hid_own_ref[...]
+    hid[0, 0, 0] = hid_ref[z]
     hid_z = [
         send(remote(hid_ref.at[lax.rem(z + j, depth)], hid.at[0, 0, j], hz_sem, j, z_dev(j)))
         for j in range(1, depth)
@@ -366,6 +366,12 @@
         copy.wait_send()
 
 
+def hand_over(*refs):
+    half = len(refs) // 2
+    for source, target in zip(refs[:half], refs[half:]):
+        target[...] = source[...]
+
+
 def fast_shards(
     activations,
     cotangent,
@@ -392,7 +398,6 @@
     hidden = decode_hidden.reshape(steps, -1)
     mine = lax.dynamic_slice_in_dim(hidden, lax.axis_index("tp") * width, width, 1)
     mine = mine.reshape(steps, depth, chunk).transpose(1, 0, 2).astype(F32)
-    own_hidden = lax.dynamic_index_in_dim(mine, lax.axis_index("grp") // 4, 0, keepdims=False)
     q_pad = -(-GQA * steps // 16) * 16
     vmem = pl.BlockSpec(memory_space=pltpu.VMEM)
     anywhere = pl.BlockSpec(memory_space=pl.ANY)
@@ -409,7 +414,7 @@
             jax.ShapeDtypeStruct((steps, kv_cols), BF16),
             jax.ShapeDtypeStruct((steps, queries.shape[2]), BF16),
         ),
-        in_specs=[vmem] * 11 + [anywhere, anywhere, smem, anywhere],
+        in_specs=[vmem] * 10 + [anywhere, anywhere, smem, anywhere],
         out_specs=(vmem,) * 6,
         scratch_shapes=[
             pltpu.VMEM((depth, 2, 2, own, kw), F32),
@@ -464,7 +469,6 @@
         moment_one[0],
         moment_two[0],
         mine,
-        own_hidden,
         hidden,
         queries[0],
         cache_keys[0],
@@ -472,6 +476,12 @@
         cache_len,
         value_weight,
     )
+    outs = pl.pallas_call(
+        hand_over,
+        out_shape=tuple(jax.ShapeDtypeStruct(out.shape, out.dtype) for out in outs),
+        in_specs=[vmem] * 6,
+        out_specs=(vmem,) * 6,
+    )(*outs)
     return tuple(out[None] for out in outs)
 
 

time: 56.8 us -> 49.2 us (0.87)
  local copies, waits for them, and re-layouts: 10.3 us -> 0.74 us
  Pallas kernels: 44.2 us -> 46.3 us
    unnamed x6 -> x0, local copies, waits for them, and re-layouts: 8.95 us -> none
    pallas_call x0 -> x1, Pallas kernels: none -> 2.15 us  [fast_shards(): pl.pallas_call(hand_over, out_shape=tuple((jax.ShapeDtypeStruct(out.shape...]
    squeeze x1 -> x0, local copies, waits for them, and re-layouts: 0.6 us -> none  [fast_shards(): lax.dynamic_index_in_dim(mine, lax.axis_index('grp') // 4, 0, keepdims=Fa...]
where the time goes in v2:
time: 49.2 us; the launch traced here: 48.9 us
  Pallas kernels  46.3 us (94%)
  between operations  1.29 us (3%)
  local copies, waits for them, and re-layouts  0.74 us (2%)
  other arithmetic  0.62 us (1%)
    pallas_call x1, Pallas kernels, fast_shards(): pl.pallas_call(functools.partial(fused, (groups, tps, steps)), out_shape=...  44.1 us
    pallas_call x1, Pallas kernels, fast_shards(): pl.pallas_call(hand_over, out_shape=tuple((jax.ShapeDtypeStruct(out.shape...  2.15 us

profile of v2, /device:TPU:0, one launch (start us, length us, event | category | flops | bytes accessed | tf_op | source)
XLA Modules:
  0.0 48.9 jit_solution(18358073764630464942)
XLA Ops:
  1.3 0.7 %constant_dynamic-slice_fusion = bf16[1,4,2560]{2,1,0:T(4,128)(2,1)S(1)} fusion(bf16[1,4,5120]{2,1,0:T(4,128)(2,1)} %param.20, s32[]{:T(128)S(6)} %select_n.3), kind=kLoop, calls=%fused_computation.1 | loop fusion | bytes 40964 | tf_op jit(solution)/shard_map/dynamic_slice | solution.py:399
  2.0 0.6 %convert_bitcast_fusion.hid_ref = f32[4,4,640]{2,1,0:T(4,128)} fusion(bf16[4,4,640]{2,0,1:T(4,128)(2,1)S(1)} %bitcast.25), kind=kLoop, calls=%fused_computation | loop fusion | flops 10240 | bytes 61440 | tf_op jit(solution)/shard_map/convert_element_type | solution.py:400
  2.6 44.1 %shard_map.172 = (f32[160,512]{1,0:T(8,128)}, f32[160,512]{1,0:T(8,128)}, f32[160,512]{1,0:T(8,128)}, bf16[4,256]{1,0:T(4,128)(2,1)}, bf16[4,256]{1,0:T(4,128)(2,1)}, /*index=5*/bf16[4,1280]{1,0:T(4,128)(2,1)}) custom-call(bf16[256,2560]{1,0:T(8,128)(2,1)} %act_ref.1, bf16[256,512]{1,0:T(8,128)(2,1)} %cot_ref.1, s32[1,16]{1,0:T(1,128)} %bitcast.27, ...), custom_call_target="tpu_custom_call" | custom-call | flops 671088640 | bytes 10485760 | tf_op jit(solution)/shard_map/pallas_call | solution.py:407
  46.8 2.2 %shard_map.173 = (f32[160,512]{1,0:T(8,128)}, f32[160,512]{1,0:T(8,128)}, f32[160,512]{1,0:T(8,128)}, bf16[4,256]{1,0:T(4,128)(2,1)}, bf16[4,256]{1,0:T(4,128)(2,1)}, /*index=5*/bf16[4,1280]{1,0:T(4,128)(2,1)}) custom-call(f32[160,512]{1,0:T(8,128)} %get-tuple-element.18.refs_0_, f32[160,512]{1,0:T(8,128)} %get-tuple-element.19.refs_1_, ...), custom_call_target="tpu_custom_call" | custom-call | tf_op jit(solution)/shard_map/pallas_call | solution.py:479
